TPU v7x, 32 devices: a whole 2x2x4 slice. The times are simulated.
32 devices in a mesh: seq: 8 (over y, x, core), exp: 4 (over z).
Axes of the slice: x: 2, y: 2, z: 4, core: 2. Of those that a mesh axis runs over, the one named last changes fastest.
Arguments:
- query_proj: bfloat16 [512, 4096], P('seq', 'exp'), may hold values from -6 to 6
- key_proj: bfloat16 [512, 4096], P('seq', 'exp'), may hold values from -6 to 6
- value_proj: bfloat16 [512, 4096], P('seq', 'exp'), may hold values from -6 to 6
- residual: bfloat16 [512, 6144], P(('seq', 'exp')), may hold values from -6 to 6
- out_weight: bfloat16 [6144, 4096], P('seq', 'exp'), may hold values from -0.09375 to 0.09375
- expert_ids: int32 [512, 2], P(('seq', 'exp')), may hold values from 0 to 3, all different within a row; in each aligned block of 16 rows (0 to 15, 16 to 31, ...) at most 12 rows name the same one
- gate_values: float32 [512, 2], P(('seq', 'exp')), may hold values from 0.2 to 1
- w_gate: bfloat16 [4, 9216, 6144], P('exp', 'seq'), may hold values from -0.078125 to 0.078125
- w_up: bfloat16 [4, 9216, 6144], P('exp', 'seq'), may hold values from -0.078125 to 0.078125
- w_down: bfloat16 [4, 9216, 6144], P('exp', 'seq'), may hold values from -0.0625 to 0.0625
Outputs:
- mixed: bfloat16 [512, 6144], P(('seq', 'exp'))
Inputs may be any that keep to these rules, and one draw needn't show every extreme that they name: `expert_ids`: within the 16 rows of one device no expert is named more than 12 times, a bound that some block reaches; the 2 experts of a row differ.
All inputs are finite; a program needn't handle non-finite values.
Results may differ from a plain program's by a relative error of at most 0.018.
Values may be sent and summed in bfloat16 or wider, within the bound.
A program may use at most 128 MiB of HBM per device.

v0:
```python
import jax
import jax.numpy as jnp
from jax import lax
from jax.sharding import PartitionSpec as P

HD = 128
TOP = 2


def entering(array, axis, combine, identity):
    devices, place = (lax.axis_size(axis), lax.axis_index(axis))
    everything = lax.all_gather(array.astype(jnp.bfloat16), axis)
    start = jnp.broadcast_to(jnp.asarray(identity, array.dtype), array.shape)

    def hop(k, before):
        reached = k < place
        new = combine(before, everything[k].astype(array.dtype))
        return jnp.where(reached, new, before)

    return lax.fori_loop(0, devices, hop, start)


def features(x):
    widened = x.astype(jnp.float32)
    return (widened * jax.nn.sigmoid(widened)).astype(jnp.bfloat16)


def times_rows(left, right):
    return lax.dot_general(
        left, right, (((1,), (1,)), ((), ())), preferred_element_type=jnp.float32
    )


def local(
    query_proj,
    key_proj,
    value_proj,
    residual,
    out_weight,
    expert_ids,
    gate_values,
    w_gate,
    w_up,
    w_down,
):
    tokens_here = query_proj.shape[0]
    heads_here = query_proj.shape[1] // HD
    query_feat = features(query_proj).reshape(tokens_here, heads_here, HD)
    key_feat = features(key_proj).reshape(tokens_here, heads_here, HD)
    value_rows = value_proj.reshape(tokens_here, heads_here, HD)
    span_state = jnp.einsum(
        "thd,the->hde", key_feat, value_rows, preferred_element_type=jnp.float32
    )
    earlier = entering(span_state, "seq", lambda a, b: a + b, jnp.zeros_like(span_state))
    prefix = earlier.astype(jnp.bfloat16)
    earlier_term = jnp.einsum(
        "thd,hde->the", query_feat, prefix, preferred_element_type=jnp.float32
    )
    scores = jnp.einsum("thd,shd->hts", query_feat, key_feat, preferred_element_type=jnp.float32)
    causal = jnp.arange(tokens_here)[:, None] >= jnp.arange(tokens_here)[None, :]
    weights = jnp.where(causal[None], scores, 0.0).astype(jnp.bfloat16)
    local_term = jnp.einsum("hts,she->the", weights, value_rows, preferred_element_type=jnp.float32)
    combined = local_term + earlier_term
    normed = combined * lax.rsqrt(jnp.mean(combined * combined, axis=-1, keepdims=True) + 1e-06)
    normed = normed.astype(jnp.bfloat16).reshape(tokens_here, heads_here * HD)
    partial_out = times_rows(normed, lax.all_gather(out_weight, "seq", axis=0, tiled=True))
    summed = lax.psum_scatter(
        partial_out.astype(jnp.bfloat16), "exp", scatter_dimension=0, tiled=True
    ).astype(jnp.float32)
    mixed_in = (residual.astype(jnp.float32) + summed).astype(jnp.bfloat16)
    groups = lax.axis_size("exp")
    tok_sub = residual.shape[0]
    capacity = max(2, (3 * tok_sub * TOP + 2 * groups - 1) // (2 * groups))
    local_rows = groups * capacity
    chosen = expert_ids.reshape(-1)
    onehot = (chosen[:, None] == jnp.arange(groups, dtype=jnp.int32)[None, :]).astype(jnp.int32)
    before = jnp.cumsum(onehot, axis=0) - onehot
    slot_index = jnp.sum(before * onehot, axis=1)
    target = chosen * capacity + slot_index
    targets = target.reshape(tok_sub, TOP)
    slot_ids = jnp.arange(local_rows, dtype=jnp.int32)
    placing = jnp.any(slot_ids[:, None, None] == targets[None, :, :], axis=2).astype(jnp.bfloat16)
    outgoing = jnp.dot(placing, mixed_in, preferred_element_type=jnp.float32).astype(jnp.bfloat16)
    outgoing = outgoing.reshape(groups, capacity, -1)
    gate_local = w_gate[0]
    up_local = w_up[0]
    down_local = w_down[0]
    hidden_here = gate_local.shape[0]
    arrived = lax.all_to_all(outgoing, "exp", split_axis=0, concat_axis=0, tiled=True).reshape(
        local_rows, -1
    )
    rows_part = lax.all_gather(arrived, "seq", axis=0, tiled=True)
    acts = jnp.concatenate(
        [times_rows(rows_part, gate_local), times_rows(rows_part, up_local)], axis=1
    )
    gate_act = acts[:, :hidden_here]
    up_act = acts[:, hidden_here:]
    activated = (jax.nn.silu(gate_act) * up_act).astype(jnp.bfloat16)
    rows_part = activated
    expert_sums = lax.psum_scatter(
        jnp.dot(rows_part, down_local, preferred_element_type=jnp.float32).astype(jnp.bfloat16),
        "seq",
        scatter_dimension=0,
        tiled=True,
    )
    expert_out = expert_sums.reshape(groups, capacity, -1)
    returned = lax.all_to_all(expert_out, "exp", split_axis=0, concat_axis=0, tiled=True).reshape(
        local_rows, -1
    )
    picked = returned[target].astype(jnp.float32).reshape(tok_sub, TOP, -1)
    mixed = mixed_in.astype(jnp.float32) + jnp.sum(gate_values[:, :, None] * picked, axis=1)
    return mixed.astype(jnp.bfloat16)


def solution(mesh):
    return jax.shard_map(
        local,
        mesh=mesh,
        in_specs=(
            P("seq", "exp"),
            P("seq", "exp"),
            P("seq", "exp"),
            P(("seq", "exp"), None),
            P("seq", "exp"),
            P(("seq", "exp"), None),
            P(("seq", "exp"), None),
            P("exp", "seq", None),
            P("exp", "seq", None),
            P("exp", "seq", None),
        ),
        out_specs=P(("seq", "exp"), None),
        check_vma=False,
    )
```

profile of v0, /device:TPU:0, one launch (start us, length us, event | category | flops | bytes accessed | tf_op | source)
XLA Modules:
  0.0 334.6 jit_solution(14853857434425266002)
XLA Ops:
  6.5 1.1 fusion.35
  7.7 1.0 convolution_convert_fusion.2
  8.7 0.0 all-gather.5.cloned.1.call-start
  8.8 0.7 all-gather.5.cloned.1.call-update
  9.6 0.3 convolution_bitcast_fusion.1
  9.9 30.0 %all-gather.9.cloned.1.call-done = bf16[64,128,128]{2,1,0:T(8,128)(2,1)} async-done(((bf16[8,128,128]{2,1,0:T(8,128)(2,1)}), bf16[64,128,128]{2,1,0:T(8,128)(2,1)}) %all-gather.9.cloned.1.call-update) | async-done | bytes 2097168 | tf_op jit(solution)/shard_map/all_gather | solution.py:12
  39.9 10.1 %while.14 = (s32[]{:T(128)}, f32[8,128,128]{2,1,0:T(8,128)S(1)}, s32[]{:T(128)}, bf16[8,8,128,128]{3,2,1,0:T(8,128)(2,1)}, s32[]{:T(128)}, /*index=5*/s32[]{:T(128)}) while((s32[]{:T(128)}, f32[8,128,128]{2,1,0:T(8,128)S(1)}, s32[]{:T(128)}, bf16[8,8,128,128]{3,2,1,0:T(8,128)(2,1)}, s32[]{:T(128)}, /*index=5*/s32[]{:T(128)}) %tuple.48), condition=%wide.region_1.2_spmd.clone, body=%wide.region_0.1_spmd.clone.sunk | while | flops 524292 | bytes 1310813 | solution.py:20
  39.9 1.2 add_select_fusion.2
  41.1 1.2 add_select_fusion.2
  42.4 1.2 add_select_fusion.2
  43.6 1.2 add_select_fusion.2
  44.9 1.2 add_select_fusion.2
  46.2 1.2 add_select_fusion.2
  47.4 1.3 add_select_fusion.2
  48.7 1.3 add_select_fusion.2
  50.0 0.3 multiply_reduce_fusion.1
  50.3 63.6 %all-gather.5.cloned.1.call-done = bf16[6144,1024]{1,0:T(8,128)(2,1)} async-done(((bf16[768,1024]{1,0:T(8,128)(2,1)}), bf16[6144,1024]{1,0:T(8,128)(2,1)}) %all-gather.5.cloned.1.call-update) | async-done | bytes 12582928 | tf_op jit(solution)/shard_map/all_gather | solution.py:66
  113.9 9.5 %convolution_convert_fusion = bf16[64,6144]{1,0:T(8,128)(2,1)} fusion(bf16[6144,1024]{1,0:T(8,128)(2,1)} %all-gather.5.cloned.1.call-done, f32[64,8,128]{2,0,1:T(8,128)S(1)} %get-tuple-element.111, f32[64,8]{0,1:T(8,128)S(1)} %add_rsqrt_fusion), kind=kOutput, calls=%fused_computation.9 | convolution fusion | flops 805830656 | bytes 13633536 | tf_op jit(solution)/shard_map/dot_general | solution.py:29
  123.5 0.0 all-gather.7.cloned.1.call-start
  123.5 0.1 copy.44
  123.6 0.1 eq.29
  123.7 0.1 fusion.57
  123.8 0.1 reduce_window_sum.11
  123.8 0.2 select_reduce_fusion
  124.0 0.1 reduce_sum.33
  124.1 0.6 broadcast_multiply_fusion
  124.7 0.1 copy.46
  124.8 0.1 fusion.58
  124.9 22.0 %reduce-scatter.3.cloned.1.call-done = bf16[16,6144]{1,0:T(8,128)(2,1)} async-done(((bf16[64,6144]{1,0:T(8,128)(2,1)}), bf16[16,6144]{1,0:T(8,128)(2,1)}) %reduce-scatter.3.cloned.1.call-update) | async-done | bytes 196624 | tf_op jit(solution)/shard_map/reduce_scatter | solution.py:67
  146.9 1.3 convolution_convert_fusion.1
  148.2 0.1 reshape.91
  148.4 22.6 %all_to_all.10 = bf16[4,12,6144]{2,1,0:T(8,128)(2,1)S(1)} all-to-all(bf16[4,12,6144]{2,1,0:T(8,128)(2,1)S(1)} %reshape.91), channel_id=1, replica_groups=mesh['seq'=8,'exp'=4] {'exp'}, dimensions={0} | all-to-all | bytes 1179648 | tf_op jit(solution)/shard_map/all_to_all | solution.py:89
  170.9 1.0 reshape.92
  171.9 0.2 reduce-scatter.5.cloned.1.call-start
  172.1 37.9 %all-gather.7.cloned.1.call-done = bf16[384,6144]{1,0:T(8,128)(2,1)} async-done(((bf16[48,6144]{1,0:T(8,128)(2,1)}), bf16[384,6144]{1,0:T(8,128)(2,1)}) %all-gather.7.cloned.1.call-update) | async-done | bytes 4718608 | tf_op jit(solution)/shard_map/all_gather | solution.py:92
  210.1 10.2 %fusion.4 = f32[384,1152]{1,0:T(8,128)S(1)} fusion(bf16[384,6144]{1,0:T(8,128)(2,1)} %all-gather.7.cloned.1.call-done, bf16[1,1152,6144]{2,1,0:T(8,128)(2,1)} %param.19), kind=kOutput, calls=%fused_computation.6 | convolution fusion | flops 5435817984 | bytes 20643840 | tf_op jit(solution)/shard_map/dot_general | solution.py:29
  220.3 23.4 %fusion.6 = bf16[384,6144]{1,0:T(8,128)(2,1)} fusion(bf16[1,1152,6144]{2,1,0:T(8,128)(2,1)} %param.21, bf16[384,6144]{1,0:T(8,128)(2,1)} %all-gather.7.cloned.1.call-done, bf16[1,1152,6144]{2,1,0:T(8,128)(2,1)} %param.20, f32[384,1152]{1,0:T(8,128)S(1)} %fusion.4), kind=kOutput, calls=%fused_computation.8 | convolution fusion | flops 10876649472 | bytes 39518208 | tf_op jit(solution)/shard_map/dot_general | solution.py:101
  243.8 54.1 %reduce-scatter.5.cloned.1.call-done = bf16[48,6144]{1,0:T(8,128)(2,1)} async-done(((bf16[384,6144]{1,0:T(8,128)(2,1)}), bf16[48,6144]{1,0:T(8,128)(2,1)}) %reduce-scatter.5.cloned.1.call-update) | async-done | bytes 589840 | tf_op jit(solution)/shard_map/reduce_scatter | solution.py:100
  297.9 2.1 reshape.93
  300.0 4.7 %all-to-all-start.1 = ((bf16[4,12,6144]{2,1,0:T(8,128)(2,1)}), bf16[4,12,6144]{2,1,0:T(8,128)(2,1)S(1)}, u32[]{:S(2)}, u32[]{:S(2)}) async-start(bf16[4,12,6144]{2,1,0:T(8,128)(2,1)} %reshape.93), calls=%async_computation.3 | async-start | bytes 1572864 | tf_op jit(solution)/shard_map/all_to_all | solution.py:107
  304.7 0.1 mul.64
  304.8 0.1 copy.43
  304.9 19.9 %all-to-all-done.1 = bf16[4,12,6144]{2,1,0:T(8,128)(2,1)S(1)} async-done(((bf16[4,12,6144]{2,1,0:T(8,128)(2,1)}), bf16[4,12,6144]{2,1,0:T(8,128)(2,1)S(1)}, u32[]{:S(2)}, u32[]{:S(2)}) %all-to-all-start.1) | async-done | bytes 589856 | tf_op jit(solution)/shard_map/all_to_all | solution.py:107
  324.8 0.1 reshape.94
  325.0 0.8 gather_fusion
  325.8 0.5 reshape.96
  326.3 1.1 multiply_reduce_fusion
  327.4 0.7 add_convert_fusion
  (31 shorter events, 0.2 us)
Async XLA Ops:
  6.5 1.2 copy-start
  6.5 33.3 %all-gather.9.cloned.1.call-start = ((), (), s32[]{:S(2)}) async-start(), calls=%async_computation.8 | async-start | bytes 2359296 | tf_op jit(solution)/shard_map/all_gather | solution.py:12
  8.7 105.2 %all-gather.5.cloned.1.call-start = ((), (), s32[]{:S(2)}) async-start(), calls=%async_computation.4 | async-start | bytes 14155776 | tf_op jit(solution)/shard_map/all_gather | solution.py:66
  9.5 137.4 %reduce-scatter.3.cloned.1.call-start = ((), (), s32[]{:S(2)}) async-start(), calls=%async_computation.5 | async-start | bytes 983040 | tf_op jit(solution)/shard_map/reduce_scatter | solution.py:67
  113.9 9.6 %copy-start.8 = (s32[16,2]{0,1:T(2,128)S(1)}, s32[16,2]{0,1:T(2,128)}, u32[]{:S(2)}) copy-start(s32[16,2]{0,1:T(2,128)} %param.17) | copy-start | bytes 388
  113.9 33.0 %copy-start.2 = (bf16[16,6144]{1,0:T(8,128)(2,1)S(1)}, bf16[16,6144]{1,0:T(8,128)(2,1)}, u32[]{:S(2)}) copy-start(bf16[16,6144]{1,0:T(8,128)(2,1)} %param.15) | copy-start | bytes 589828
  123.5 86.6 %all-gather.7.cloned.1.call-start = ((), (), s32[]{:S(2)}) async-start(), calls=%async_computation.6 | async-start | bytes 5308416 | tf_op jit(solution)/shard_map/all_gather | solution.py:92
  124.0 96.3 %copy-start.6 = (s32[32]{0:T(128)}, s32[32]{0:T(128)S(1)}, u32[]{:S(2)}) copy-start(s32[32]{0:T(128)S(1)} %select_reduce_fusion) | copy-start | bytes 388
  171.9 125.9 %reduce-scatter.5.cloned.1.call-start = ((), (), s32[]{:S(2)}) async-start(), calls=%async_computation.7 | async-start | bytes 5308416 | tf_op jit(solution)/shard_map/reduce_scatter | solution.py:100
  243.8 60.9 %copy-start.5 = (s32[16,2]{1,0:T(8,128)S(1)}, s32[16,2]{1,0:T(8,128)}, u32[]{:S(2)}) copy-start(s32[16,2]{1,0:T(8,128)} %get-tuple-element.108) | copy-start | bytes 388
  243.8 61.0 %copy-start.9 = (f32[16,2]{0,1:T(2,128)S(1)}, f32[16,2]{0,1:T(2,128)}, u32[]{:S(2)}) copy-start(f32[16,2]{0,1:T(2,128)} %param.18) | copy-start | bytes 388
  243.8 61.1 %copy-start.7 = (s32[32]{0:T(128)S(1)}, s32[32]{0:T(128)}, u32[]{:S(2)}) copy-start(s32[32]{0:T(128)} %copy-done.6) | copy-start | bytes 388
  297.9 30.2 %copy-start.1 = (bf16[64,1024]{1,0:T(8,128)(2,1)S(1)}, bf16[64,1024]{1,0:T(8,128)(2,1)}, u32[]{:S(2)}) copy-start(bf16[64,1024]{1,0:T(8,128)(2,1)} %param.14) | copy-start | bytes 393220
  300.0 27.4 %copy-start.3 = (bf16[16,6144]{1,0:T(8,128)(2,1)S(1)}, bf16[16,6144]{1,0:T(8,128)(2,1)}, u32[]{:S(2)}) copy-start(bf16[16,6144]{1,0:T(8,128)(2,1)} %param.15) | copy-start | bytes 589828
  300.0 27.4 %copy-start.4 = (bf16[16,6144]{1,0:T(8,128)(2,1)S(1)}, bf16[16,6144]{1,0:T(8,128)(2,1)}, u32[]{:S(2)}) copy-start(bf16[16,6144]{1,0:T(8,128)(2,1)} %reduce-scatter.3.cloned.1.call-done) | copy-start | bytes 589828
  300.0 24.8 %all-to-all-start.1 = ((bf16[4,12,6144]{2,1,0:T(8,128)(2,1)}), bf16[4,12,6144]{2,1,0:T(8,128)(2,1)S(1)}, u32[]{:S(2)}, u32[]{:S(2)}) async-start(bf16[4,12,6144]{2,1,0:T(8,128)(2,1)} %reshape.93), calls=%async_computation.3 | async-start | bytes 1572864 | tf_op jit(solution)/shard_map/all_to_all | solution.py:107
Sparse Core Ops, SparseCore 0:
  9.2 30.5 all-gather.8
  41.8 72.1 all-gather.4
  123.6 23.2 reduce-scatter.2
  172.0 38.0 all-gather.6
  243.9 53.8 reduce-scatter.4
where the time goes:
time: 335 us
  waiting for transfers between devices  228 us (68%)
  matrix products  46.1 us (14%)
  blocking collectives  22.6 us (7%)
  other arithmetic  14 us (4%)
  between operations  13.3 us (4%)
  local copies, waits for them, and re-layouts  5.18 us (2%)
  starting transfers between devices  5.07 us (2%)
    all_gather x1, waiting for transfers between devices, local(): lax.all_gather(out_weight, 'seq', axis=0, tiled=True)  63.6 us
    reduce_scatter x1, waiting for transfers between devices, local(): lax.psum_scatter(jnp.dot(rows_part, down_local, preferred_element_type=jn...  54.1 us
    all_gather x1, waiting for transfers between devices, local(): rows_part = lax.all_gather(arrived, 'seq', axis=0, tiled=True)  37.9 us
    all_gather x1, waiting for transfers between devices, entering(): everything = lax.all_gather(array.astype(jnp.bfloat16), axis)  30 us
    dot_general x1, matrix products, local(): jnp.dot(rows_part, down_local, preferred_element_type=jnp.float32)  23.4 us
    all_to_all x1, blocking collectives, local(): lax.all_to_all(outgoing, 'exp', split_axis=0, concat_axis=0, tiled=True)  22.6 us
    reduce_scatter x1, waiting for transfers between devices, local(): lax.psum_scatter(partial_out.astype(jnp.bfloat16), 'exp', scatter_dimensi...  22 us
    all_to_all x1, waiting for transfers between devices, local(): lax.all_to_all(expert_out, 'exp', split_axis=0, concat_axis=0, tiled=True)  19.9 us
  transfers between devices with their start and end apart: 6, of which 6 were waited for; matrix products, arithmetic and copies ran while one was open for 4% of the time, Pallas kernels for 0%

commit v1 on v0

--- a/solution.py
+++ b/solution.py
@@ -63,7 +63,33 @@
     combined = local_term + earlier_term
     normed = combined * lax.rsqrt(jnp.mean(combined * combined, axis=-1, keepdims=True) + 1e-06)
     normed = normed.astype(jnp.bfloat16).reshape(tokens_here, heads_here * HD)
-    partial_out = times_rows(normed, lax.all_gather(out_weight, "seq", axis=0, tiled=True))
+
+    def view_series_all(z_in, axis_key):
+        view_out = lax.axis_size(axis_key)
+        z = lax.axis_index(axis_key)
+        mid_arr, e_now, block_next = (view_out, z, z_in.shape[0])
+        kept_rows = tuple((c * mid_arr if u == 0 else c for u, c in enumerate(z_in.shape)))
+        tmp = jnp.zeros(kept_rows, z_in.dtype)
+        opened = lax.dynamic_update_slice_in_dim(tmp, z_in, e_now * block_next, axis=0)
+        local_part = base_arr = z_in
+        tick = 1
+        while tick < mid_arr // 2 + 1:
+            local_part = lax.ppermute(
+                local_part, axis_key, tuple(((u, (u + 1) % mid_arr) for u in range(mid_arr)))
+            )
+            opened = lax.dynamic_update_slice_in_dim(
+                opened, local_part, (e_now - tick) % mid_arr * block_next, axis=0
+            )
+            if 2 * tick < mid_arr:
+                tile_out = tuple(((u, (u - 1) % mid_arr) for u in range(mid_arr)))
+                base_arr = lax.ppermute(base_arr, axis_key, tile_out)
+                opened = lax.dynamic_update_slice_in_dim(
+                    opened, base_arr, (e_now + tick) % mid_arr * block_next, axis=0
+                )
+            tick = tick + 1
+        return opened
+
+    partial_out = times_rows(normed, view_series_all(out_weight, axis_key="seq"))
     summed = lax.psum_scatter(
         partial_out.astype(jnp.bfloat16), "exp", scatter_dimension=0, tiled=True
     ).astype(jnp.float32)

time: 335 us -> 366 us (1.093)
  local copies, waits for them, and re-layouts: 5.18 us -> 30.1 us
  starting transfers between devices: 5.07 us -> 14.2 us
    ppermute x0 -> x7, waiting for transfers between devices: none -> 87.1 us  [the longest x4 73.2 us: view_series_all(): lax.ppermute(local_part, axis_key, tuple(((u, (u + 1) % mid_arr) for u in...]
    all_gather x1 -> x0, waiting for transfers between devices: 63.6 us -> none  [local(): lax.all_gather(out_weight, 'seq', axis=0, tiled=True)]
    all_gather x1, waiting for transfers between devices: 30 us -> 0.01 us  [entering(): everything = lax.all_gather(array.astype(jnp.bfloat16), axis)]
    dynamic_update_slice x0 -> x8, local copies, waits for them, and re-layouts: none -> 18.7 us  [the longest x4 10.8 us: view_series_all(): lax.dynamic_update_slice_in_dim(opened, local_part, (e_now - tick) % mid_...]
    ppermute x0 -> x7, starting transfers between devices: none -> 9.32 us  [the longest x3 8.45 us: view_series_all(): base_arr = lax.ppermute(base_arr, axis_key, tile_out)]
    broadcast_in_dim x0 -> x1, local copies, waits for them, and re-layouts: none -> 6.14 us  [view_series_all(): tmp = jnp.zeros(kept_rows, z_in.dtype)]
  transfers between devices with their start and end apart: 6 -> 12, of which waited for: 6 -> 10; matrix products, arithmetic and copies ran while one was open for 4% -> 10% of each run, Pallas kernels for 0% -> 0%
where the time goes in v1:
time: 366 us; the launch traced here: 365 us
  waiting for transfers between devices  225 us (61%)
  matrix products  46.1 us (13%)
  local copies, waits for them, and re-layouts  30.1 us (8%)
  blocking collectives  22.6 us (6%)
  starting transfers between devices  14.2 us (4%)
  other arithmetic  13.9 us (4%)
  between operations  13.3 us (4%)
    ppermute x4, waiting for transfers between devices, view_series_all(): lax.ppermute(local_part, axis_key, tuple(((u, (u + 1) % mid_arr) for u in...  73.2 us
    reduce_scatter x1, waiting for transfers between devices, local(): lax.psum_scatter(jnp.dot(rows_part, down_local, preferred_element_type=jn...  54.1 us
    all_gather x1, waiting for transfers between devices, local(): rows_part = lax.all_gather(arrived, 'seq', axis=0, tiled=True)  37.9 us
    reduce_scatter x1, waiting for transfers between devices, local(): lax.psum_scatter(partial_out.astype(jnp.bfloat16), 'exp', scatter_dimensi...  25.5 us
    dot_general x1, matrix products, local(): jnp.dot(rows_part, down_local, preferred_element_type=jnp.float32)  23.4 us
    all_to_all x1, blocking collectives, local(): lax.all_to_all(outgoing, 'exp', split_axis=0, concat_axis=0, tiled=True)  22.6 us
    all_to_all x1, waiting for transfers between devices, local(): lax.all_to_all(expert_out, 'exp', split_axis=0, concat_axis=0, tiled=True)  19.9 us
    dot_general x2, matrix products, times_rows(): lax.dot_general(left, right, (((1,), (1,)), ((), ())), preferred_element_...  19.7 us
  transfers between devices with their start and end apart: 12, of which 10 were waited for; matrix products, arithmetic and copies ran while one was open for 10% of the time, Pallas kernels for 0%

profile of v1, /device:TPU:0, one launch (start us, length us, event | category | flops | bytes accessed | tf_op | source)
XLA Modules:
  0.0 364.8 jit_solution(7598408187239935435)
XLA Ops:
  6.5 0.5 collective-permute-start
  7.0 1.2 fusion.35
  8.2 1.0 convolution_convert_fusion.2
  9.3 3.0 collective-permute-start.1
  12.3 36.5 %collective-permute-done = bf16[768,1024]{1,0:T(8,128)(2,1)} collective-permute-done((bf16[768,1024]{1,0:T(8,128)(2,1)}, bf16[768,1024]{1,0:T(8,128)(2,1)}, u32[]{:S(2)}, u32[]{:S(2)}) %collective-permute-start) | collective-permute-done | bytes 1572896 | tf_op jit(solution)/shard_map/ppermute | solution.py:77
  48.7 0.4 collective-permute-start.2
  49.1 3.4 collective-permute-done.1
  52.5 2.8 collective-permute-start.3
  55.3 28.0 %collective-permute-done.2 = bf16[768,1024]{1,0:T(8,128)(2,1)} collective-permute-done((bf16[768,1024]{1,0:T(8,128)(2,1)}, bf16[768,1024]{1,0:T(8,128)(2,1)}, u32[]{:S(2)}, u32[]{:S(2)}) %collective-permute-start.2) | collective-permute-done | bytes 1572896 | tf_op jit(solution)/shard_map/ppermute | solution.py:77
  83.3 6.1 %broadcast_in_dim.29 = bf16[6144,1024]{1,0:T(8,128)(2,1)} broadcast(bf16[]{:T(256)} %constant.95.clone.1), dimensions={} | broadcast | bytes 12582914 | tf_op jit(solution)/shard_map/broadcast_in_dim | solution.py:72
  89.5 1.3 constant_dynamic-update-slice_fusion.7
  91.1 2.7 constant_dynamic-update-slice_fusion.6
  93.8 2.7 constant_dynamic-update-slice_fusion.5
  96.4 2.6 collective-permute-start.5
  99.1 2.7 constant_dynamic-update-slice_fusion.4
  101.8 2.7 constant_dynamic-update-slice_fusion.3
  104.4 2.9 collective-permute-done.4
  107.3 10.0 %while.14 = (s32[]{:T(128)}, f32[8,128,128]{2,1,0:T(8,128)S(1)}, s32[]{:T(128)}, bf16[8,8,128,128]{3,2,1,0:T(8,128)(2,1)}, s32[]{:T(128)}, /*index=5*/s32[]{:T(128)}) while((s32[]{:T(128)}, f32[8,128,128]{2,1,0:T(8,128)S(1)}, s32[]{:T(128)}, bf16[8,8,128,128]{3,2,1,0:T(8,128)(2,1)}, s32[]{:T(128)}, /*index=5*/s32[]{:T(128)}) %tuple.46), condition=%wide.region_1.2_spmd.clone, body=%wide.region_0.1_spmd.clone.sunk | while | flops 524292 | bytes 1310813 | solution.py:20
  107.3 1.2 add_select_fusion.2
  108.5 1.2 add_select_fusion.2
  109.8 1.2 add_select_fusion.2
  111.1 1.2 add_select_fusion.2
  112.3 1.2 add_select_fusion.2
  113.6 1.2 add_select_fusion.2
  114.8 1.2 add_select_fusion.2
  116.1 1.2 add_select_fusion.2
  117.6 2.8 constant_dynamic-update-slice_fusion.2
  120.4 10.5 %collective-permute-done.5 = bf16[768,1024]{1,0:T(8,128)(2,1)S(1)} collective-permute-done((bf16[768,1024]{1,0:T(8,128)(2,1)}, bf16[768,1024]{1,0:T(8,128)(2,1)S(1)}, u32[]{:S(2)}, u32[]{:S(2)}) %collective-permute-start.5) | collective-permute-done | bytes 1572896 | tf_op jit(solution)/shard_map/ppermute | solution.py:85
  130.9 1.3 constant_dynamic-update-slice_fusion.1
  132.2 5.9 %collective-permute-done.6 = bf16[768,1024]{1,0:T(8,128)(2,1)} collective-permute-done((bf16[768,1024]{1,0:T(8,128)(2,1)}, bf16[768,1024]{1,0:T(8,128)(2,1)}, u32[]{:S(2)}, u32[]{:S(2)}) %collective-permute-start.6) | collective-permute-done | bytes 1572896 | tf_op jit(solution)/shard_map/ppermute | solution.py:77
  138.1 2.7 constant_dynamic-update-slice_fusion
  140.8 9.5 %convolution_convert_fusion = bf16[64,6144]{1,0:T(8,128)(2,1)} fusion(bf16[6144,1024]{1,0:T(8,128)(2,1)} %constant_dynamic-update-slice_fusion, f32[64,8,128]{2,0,1:T(8,128)S(1)} %get-tuple-element.111, f32[64,8]{0,1:T(8,128)S(1)} %add_rsqrt_fusion), kind=kOutput, calls=%fused_computation.9 | convolution fusion | flops 805830656 | bytes 13633536 | tf_op jit(solution)/shard_map/dot_general | solution.py:29
  150.9 0.6 broadcast_multiply_fusion
  151.7 25.5 %reduce-scatter.3.cloned.1.call-done = bf16[16,6144]{1,0:T(8,128)(2,1)} async-done(((bf16[64,6144]{1,0:T(8,128)(2,1)}), bf16[16,6144]{1,0:T(8,128)(2,1)}) %reduce-scatter.3.cloned.1.call-update) | async-done | bytes 196624 | tf_op jit(solution)/shard_map/reduce_scatter | solution.py:93
  177.2 1.3 convolution_convert_fusion.1
  178.7 22.6 %all_to_all.10 = bf16[4,12,6144]{2,1,0:T(8,128)(2,1)S(1)} all-to-all(bf16[4,12,6144]{2,1,0:T(8,128)(2,1)S(1)} %reshape.91), channel_id=1, replica_groups=mesh['seq'=8,'exp'=4] {'exp'}, dimensions={0} | all-to-all | bytes 1179648 | tf_op jit(solution)/shard_map/all_to_all | solution.py:115
  201.2 1.0 reshape.92
  202.4 37.9 %all-gather.4.cloned.1.call-done = bf16[384,6144]{1,0:T(8,128)(2,1)} async-done(((bf16[48,6144]{1,0:T(8,128)(2,1)}), bf16[384,6144]{1,0:T(8,128)(2,1)}) %all-gather.4.cloned.1.call-update) | async-done | bytes 4718608 | tf_op jit(solution)/shard_map/all_gather | solution.py:118
  240.3 10.3 %fusion.4 = f32[384,1152]{1,0:T(8,128)S(1)} fusion(bf16[384,6144]{1,0:T(8,128)(2,1)} %all-gather.4.cloned.1.call-done, bf16[1,1152,6144]{2,1,0:T(8,128)(2,1)} %param.19), kind=kOutput, calls=%fused_computation.6 | convolution fusion | flops 5435817984 | bytes 20643840 | tf_op jit(solution)/shard_map/dot_general | solution.py:29
  250.7 23.4 %fusion.6 = bf16[384,6144]{1,0:T(8,128)(2,1)} fusion(bf16[1,1152,6144]{2,1,0:T(8,128)(2,1)} %param.21, bf16[384,6144]{1,0:T(8,128)(2,1)} %all-gather.4.cloned.1.call-done, bf16[1,1152,6144]{2,1,0:T(8,128)(2,1)} %param.20, f32[384,1152]{1,0:T(8,128)S(1)} %fusion.4), kind=kOutput, calls=%fused_computation.8 | convolution fusion | flops 10876649472 | bytes 39518208 | tf_op jit(solution)/shard_map/dot_general | solution.py:127
  274.1 54.1 %reduce-scatter.5.cloned.1.call-done = bf16[48,6144]{1,0:T(8,128)(2,1)} async-done(((bf16[384,6144]{1,0:T(8,128)(2,1)}), bf16[48,6144]{1,0:T(8,128)(2,1)}) %reduce-scatter.5.cloned.1.call-update) | async-done | bytes 589840 | tf_op jit(solution)/shard_map/reduce_scatter | solution.py:126
  328.2 2.1 reshape.93
  330.3 4.6 %all-to-all-start.1 = ((bf16[4,12,6144]{2,1,0:T(8,128)(2,1)}), bf16[4,12,6144]{2,1,0:T(8,128)(2,1)S(1)}, u32[]{:S(2)}, u32[]{:S(2)}) async-start(bf16[4,12,6144]{2,1,0:T(8,128)(2,1)} %reshape.93), calls=%async_computation.3 | async-start | bytes 1572864 | tf_op jit(solution)/shard_map/all_to_all | solution.py:133
  335.1 19.9 %all-to-all-done.1 = bf16[4,12,6144]{2,1,0:T(8,128)(2,1)S(1)} async-done(((bf16[4,12,6144]{2,1,0:T(8,128)(2,1)}), bf16[4,12,6144]{2,1,0:T(8,128)(2,1)S(1)}, u32[]{:S(2)}, u32[]{:S(2)}) %all-to-all-start.1) | async-done | bytes 589856 | tf_op jit(solution)/shard_map/all_to_all | solution.py:133
  355.2 0.8 gather_fusion
  355.9 0.5 reshape.96
  356.4 1.1 multiply_reduce_fusion
  357.5 0.7 add_convert_fusion
  (53 shorter events, 2.2 us)
Async XLA Ops:
  6.5 1.7 copy-start
  6.5 82.9 %copy-start.2 = (bf16[768,1024]{1,0:T(8,128)(2,1)S(1)}, bf16[768,1024]{1,0:T(8,128)(2,1)}, u32[]{:S(2)}) copy-start(bf16[768,1024]{1,0:T(8,128)(2,1)} %param.16) | copy-start | bytes 4718596
  6.5 100.7 %all-gather.6.cloned.1.call-start = ((), (), s32[]{:S(2)}) async-start(), calls=%async_computation.7 | async-start | bytes 2359296 | tf_op jit(solution)/shard_map/all_gather | solution.py:12
  6.5 42.2 %collective-permute-start = (bf16[768,1024]{1,0:T(8,128)(2,1)}, bf16[768,1024]{1,0:T(8,128)(2,1)}, u32[]{:S(2)}, u32[]{:S(2)}) collective-permute-start(bf16[768,1024]{1,0:T(8,128)(2,1)} %param.16), channel_id=1, source_target_pairs={{0,4},{4,8},{8,12},{12,16},{16,20},{20,24},{24,28},{28,0},{1,5},{5... | collective-permute-start | bytes 4718600 | tf_op jit(solution)/shard_map/ppermute | solution.py:77
  9.2 168.0 %reduce-scatter.3.cloned.1.call-start = ((), (), s32[]{:S(2)}) async-start(), calls=%async_computation.4 | async-start | bytes 983040 | tf_op jit(solution)/shard_map/reduce_scatter | solution.py:93
  9.3 43.2 %collective-permute-start.1 = (bf16[768,1024]{1,0:T(8,128)(2,1)}, bf16[768,1024]{1,0:T(8,128)(2,1)}, u32[]{:S(2)}, u32[]{:S(2)}) collective-permute-start(bf16[768,1024]{1,0:T(8,128)(2,1)} %param.16), channel_id=1, source_target_pairs={{0,28},{4,0},{8,4},{12,8},{16,12},{20,16},{24,20},{28,24},{1,29},{... | collective-permute-start | bytes 4718600 | tf_op jit(solution)/shard_map/ppermute | solution.py:85
  48.7 34.6 %collective-permute-start.2 = (bf16[768,1024]{1,0:T(8,128)(2,1)}, bf16[768,1024]{1,0:T(8,128)(2,1)}, u32[]{:S(2)}, u32[]{:S(2)}) collective-permute-start(bf16[768,1024]{1,0:T(8,128)(2,1)} %collective-permute-done), channel_id=1, source_target_pairs={{0,4},{4,8},{8,12},{12,16},{16,20},{20,24},{24,28},{28,0},{1,5},{5... | collective-permute-start | bytes 4718600 | tf_op jit(solution)/shard_map/ppermute | solution.py:77
  52.5 44.0 %collective-permute-start.3 = (bf16[768,1024]{1,0:T(8,128)(2,1)}, bf16[768,1024]{1,0:T(8,128)(2,1)}, u32[]{:S(2)}, u32[]{:S(2)}) collective-permute-start(bf16[768,1024]{1,0:T(8,128)(2,1)} %collective-permute-done.1), channel_id=1, source_target_pairs={{0,28},{4,0},{8,4},{12,8},{16,12},{20,16},{24,20},{28,24},{1,29},{... | collective-permute-start | bytes 4718600 | tf_op jit(solution)/shard_map/ppermute | solution.py:85
  83.3 24.0 %collective-permute-start.4 = (bf16[768,1024]{1,0:T(8,128)(2,1)}, bf16[768,1024]{1,0:T(8,128)(2,1)}, u32[]{:S(2)}, u32[]{:S(2)}) collective-permute-start(bf16[768,1024]{1,0:T(8,128)(2,1)} %collective-permute-done.2), channel_id=1, source_target_pairs={{0,4},{4,8},{8,12},{12,16},{16,20},{20,24},{24,28},{28,0},{1,5},{5... | collective-permute-start | bytes 4718600 | tf_op jit(solution)/shard_map/ppermute | solution.py:77
  96.4 34.4 %collective-permute-start.5 = (bf16[768,1024]{1,0:T(8,128)(2,1)}, bf16[768,1024]{1,0:T(8,128)(2,1)S(1)}, u32[]{:S(2)}, u32[]{:S(2)}) collective-permute-start(bf16[768,1024]{1,0:T(8,128)(2,1)} %collective-permute-done.3), channel_id=1, source_target_pairs={{0,28},{4,0},{8,4},{12,8},{16,12},{20,16},{24,20},{28,24},{1,29},{... | collective-permute-start | bytes 4718600 | tf_op jit(solution)/shard_map/ppermute | solution.py:85
  107.3 30.8 %collective-permute-start.6 = (bf16[768,1024]{1,0:T(8,128)(2,1)}, bf16[768,1024]{1,0:T(8,128)(2,1)}, u32[]{:S(2)}, u32[]{:S(2)}) collective-permute-start(bf16[768,1024]{1,0:T(8,128)(2,1)} %collective-permute-done.4), channel_id=1, source_target_pairs={{0,4},{4,8},{8,12},{12,16},{16,20},{20,24},{24,28},{28,0},{1,5},{5... | collective-permute-start | bytes 4718600 | tf_op jit(solution)/shard_map/ppermute | solution.py:77
  132.2 18.1 %copy-start.9 = (s32[16,2]{0,1:T(2,128)S(1)}, s32[16,2]{0,1:T(2,128)}, u32[]{:S(2)}) copy-start(s32[16,2]{0,1:T(2,128)} %param.17) | copy-start | bytes 388
  132.2 45.0 %copy-start.3 = (bf16[16,6144]{1,0:T(8,128)(2,1)S(1)}, bf16[16,6144]{1,0:T(8,128)(2,1)}, u32[]{:S(2)}) copy-start(bf16[16,6144]{1,0:T(8,128)(2,1)} %param.15) | copy-start | bytes 589828
  150.3 90.1 %all-gather.4.cloned.1.call-start = ((), (), s32[]{:S(2)}) async-start(), calls=%async_computation.5 | async-start | bytes 5308416 | tf_op jit(solution)/shard_map/all_gather | solution.py:118
  150.8 26.4 %copy-start.7 = (s32[32]{0:T(128)}, s32[32]{0:T(128)S(1)}, u32[]{:S(2)}) copy-start(s32[32]{0:T(128)S(1)} %select_reduce_fusion) | copy-start | bytes 388
  202.2 126.0 %reduce-scatter.5.cloned.1.call-start = ((), (), s32[]{:S(2)}) async-start(), calls=%async_computation.6 | async-start | bytes 5308416 | tf_op jit(solution)/shard_map/reduce_scatter | solution.py:126
  250.6 84.3 %copy-start.6 = (s32[16,2]{1,0:T(8,128)S(1)}, s32[16,2]{1,0:T(8,128)}, u32[]{:S(2)}) copy-start(s32[16,2]{1,0:T(8,128)} %get-tuple-element.108) | copy-start | bytes 388
  250.6 84.4 %copy-start.10 = (f32[16,2]{0,1:T(2,128)S(1)}, f32[16,2]{0,1:T(2,128)}, u32[]{:S(2)}) copy-start(f32[16,2]{0,1:T(2,128)} %param.18) | copy-start | bytes 388
  250.6 84.4 %copy-start.8 = (s32[32]{0:T(128)S(1)}, s32[32]{0:T(128)}, u32[]{:S(2)}) copy-start(s32[32]{0:T(128)} %copy-done.7) | copy-start | bytes 388
  250.6 107.6 %copy-start.1 = (bf16[64,1024]{1,0:T(8,128)(2,1)S(1)}, bf16[64,1024]{1,0:T(8,128)(2,1)}, u32[]{:S(2)}) copy-start(bf16[64,1024]{1,0:T(8,128)(2,1)} %param.14) | copy-start | bytes 393220
  274.1 83.4 %copy-start.4 = (bf16[16,6144]{1,0:T(8,128)(2,1)S(1)}, bf16[16,6144]{1,0:T(8,128)(2,1)}, u32[]{:S(2)}) copy-start(bf16[16,6144]{1,0:T(8,128)(2,1)} %param.15) | copy-start | bytes 589828
  274.1 83.4 %copy-start.5 = (bf16[16,6144]{1,0:T(8,128)(2,1)S(1)}, bf16[16,6144]{1,0:T(8,128)(2,1)}, u32[]{:S(2)}) copy-start(bf16[16,6144]{1,0:T(8,128)(2,1)} %reduce-scatter.3.cloned.1.call-done) | copy-start | bytes 589828
  330.3 24.7 %all-to-all-start.1 = ((bf16[4,12,6144]{2,1,0:T(8,128)(2,1)}), bf16[4,12,6144]{2,1,0:T(8,128)(2,1)S(1)}, u32[]{:S(2)}, u32[]{:S(2)}) async-start(bf16[4,12,6144]{2,1,0:T(8,128)(2,1)} %reshape.93), calls=%async_computation.3 | async-start | bytes 1572864 | tf_op jit(solution)/shard_map/all_to_all | solution.py:133
Sparse Core Ops, SparseCore 0:
  9.3 38.9 all-gather.5
  150.4 26.7 reduce-scatter.2
  202.3 37.9 all-gather.3
  274.2 53.8 reduce-scatter.4
